TPU v7x, 32 devices: a whole 2x2x4 slice. The times are simulated.
32 devices in a mesh: groups: 2 (over x), mp: 8 (over z, y), dp: 2 (over core).
Axes of the slice: x: 2, y: 2, z: 4, core: 2. Of those that a mesh axis runs over, the one named last changes fastest.
Arguments:
- latents: bfloat16 [12, 128, 128, 320], P(('groups', 'dp'), 'mp'), parts along dimension 0, may hold values from -6 to 6
- room_labels: int32 [12, 128, 128], P(('groups', 'dp'), 'mp'), parts along dimension 0, may hold values from 0 to 15
- timesteps: int32 [12], P(('groups', 'dp')), parts along dimension 0, may hold values from 0 to 999
- label_table: bfloat16 [16, 320], replicated, may hold values from -6 to 6
- time_weight: bfloat16 [1280, 320], replicated, may hold values from -0.15625 to 0.15625
- trunk_weight: bfloat16 [320, 3, 3, 320], P('mp'), may hold values from -0.109375 to 0.109375
- control_weight: bfloat16 [320, 3, 3, 320], P('mp'), may hold values from -0.109375 to 0.109375
- mix_weight: bfloat16 [320, 320], P('mp'), may hold values from -0.3125 to 0.3125
- cotangent: bfloat16 [12, 128, 128, 320], P(('groups', 'dp'), 'mp'), parts along dimension 0, may hold values from -0.08984375 to 0.08984375
Outputs:
- output: bfloat16 [12, 128, 128, 320], P(('groups', 'dp'), 'mp'), parts along dimension 0
- grad_control: float32 [640, 3, 3, 320], P(('groups', 'mp')), parts along dimension 0
- grad_mix: float32 [640, 320], P(('groups', 'mp')), parts along dimension 0
- grad_table: float32 [32, 320], P('groups'), parts along dimension 0
There are 2 independent parts, one for each index of `groups`. A program takes and returns all parts, laid end to end along the dimension named above; an argument that names none is the same for every part. Nothing has to cross between parts.
All inputs are finite; a program needn't handle non-finite values.
Results may differ from a plain program's by a relative error of at most 0.0057.
Values may be sent and summed in bfloat16 or wider, within the bound.
A program may use at most 256 MiB of HBM per device.

v0:
```python
import math
import jax
import jax.numpy as jnp
from jax import lax
from jax.sharding import PartitionSpec as P


def with_halo(cells, sides, width):
    for axis, dim in sides:
        count = lax.axis_size(axis)
        ends = count - 1
        head = lax.slice_in_dim(cells, 0, width, axis=dim)
        tail = lax.slice_in_dim(cells, cells.shape[dim] - width, cells.shape[dim], axis=dim)
        cells = jnp.concatenate(
            [
                lax.ppermute(tail, axis, [(i, (i + 1) % count) for i in range(ends)]),
                cells,
                lax.ppermute(head, axis, [((i + 1) % count, i) for i in range(ends)]),
            ],
            axis=dim,
        )
    return cells


def sinusoid(timesteps, embed_width):
    half_width = embed_width // 2
    indices = jnp.arange(half_width, dtype=jnp.float32)
    frequency = jnp.exp(-math.log(10000.0) * indices / half_width)
    angles = timesteps.astype(jnp.float32)[:, None] * frequency[None, :]
    return jnp.concatenate([jnp.cos(angles), jnp.sin(angles)], axis=1)


def forward_taps(frame, kernel):
    row_count = frame.shape[1] - 2
    span_cols = frame.shape[2] - 2
    running = jnp.zeros(frame.shape[:1] + (row_count, span_cols, kernel.shape[3]), jnp.float32)
    for tap_row in range(3):
        for tap_col in range(3):
            running = running + jnp.einsum(
                "bhwc,cd->bhwd",
                frame[:, tap_row : tap_row + row_count, tap_col : tap_col + span_cols],
                kernel[:, tap_row, tap_col],
                preferred_element_type=jnp.float32,
            )
    return running


def backward_taps(frame, kernel):
    row_count = frame.shape[1] - 2
    span_cols = frame.shape[2] - 2
    running = jnp.zeros(frame.shape[:1] + (row_count, span_cols, kernel.shape[0]), jnp.float32)
    for tap_row in range(3):
        for tap_col in range(3):
            running = running + jnp.einsum(
                "bhwd,cd->bhwc",
                frame[
                    :, 2 - tap_row : 2 - tap_row + row_count, 2 - tap_col : 2 - tap_col + span_cols
                ],
                kernel[:, tap_row, tap_col],
                preferred_element_type=jnp.float32,
            )
    return running


def per_device(
    latents,
    room_labels,
    timesteps,
    label_table,
    time_weight,
    trunk_weight,
    control_weight,
    mix_weight,
    cotangent,
):
    images, row_count, span_cols, channels = latents.shape
    rooms = label_table.shape[0]
    onehot = (room_labels[..., None] == jnp.arange(rooms, dtype=jnp.int32)).astype(jnp.bfloat16)
    embedded = jnp.einsum("bhwr,rc->bhwc", onehot, label_table, preferred_element_type=jnp.float32)
    control_in = (latents.astype(jnp.float32) + embedded).astype(jnp.bfloat16)
    stacked = jnp.stack([latents, control_in])
    framed = with_halo(stacked, (("mp", 2),), 1)
    framed = jnp.pad(framed, ((0, 0), (0, 0), (0, 0), (1, 1), (0, 0)))
    trunk_frame = framed[0]
    control_frame = framed[1]
    time_features = jax.nn.silu(sinusoid(timesteps, time_weight.shape[0])).astype(jnp.bfloat16)
    time_shift = jnp.dot(time_features, time_weight, preferred_element_type=jnp.float32)[
        :, None, None, :
    ]
    trunk_full = lax.all_gather(trunk_weight, "mp", axis=0, tiled=True)
    trunk_pre = forward_taps(trunk_frame, trunk_full) + time_shift
    control_full, mix_full = (
        lax.all_gather(control_weight, "mp", axis=0, tiled=True),
        lax.all_gather(mix_weight, "mp", axis=0, tiled=True),
    )
    control_pre = forward_taps(control_frame, control_full) + time_shift
    gated_act = jax.nn.silu(control_pre).astype(jnp.bfloat16)
    mixed_out = jnp.einsum("bhwc,cd->bhwd", gated_act, mix_full, preferred_element_type=jnp.float32)
    output = (jax.nn.silu(trunk_pre) + mixed_out).astype(jnp.bfloat16)
    back_gate = jnp.einsum("bhwd,cd->bhwc", cotangent, mix_full, preferred_element_type=jnp.float32)
    sigmoid_val = jax.nn.sigmoid(control_pre)
    back_pre = (back_gate * sigmoid_val * (1.0 + control_pre * (1.0 - sigmoid_val))).astype(
        jnp.bfloat16
    )
    back_frame = with_halo(back_pre, (("mp", 1),), 1)
    back_frame = jnp.pad(back_frame, ((0, 0), (0, 0), (1, 1), (0, 0)))
    back_kernel = lax.all_gather(control_weight, "mp", axis=0, tiled=True)
    back_in = backward_taps(back_frame, back_kernel)
    table_local = jnp.einsum(
        "bhwr,bhwc->rc", onehot.astype(jnp.float32), back_in, precision=lax.Precision.HIGHEST
    )
    grad_table = lax.psum(table_local, ("mp", "dp"))
    pieces = []
    for tap_row in range(3):
        for tap_col in range(3):
            pieces.append(
                jnp.einsum(
                    "bhwc,bhwd->cd",
                    control_frame[:, tap_row : tap_row + row_count, tap_col : tap_col + span_cols],
                    back_pre,
                    preferred_element_type=jnp.float32,
                )
            )
    kernel_rows = jnp.stack(pieces, axis=1).reshape(channels, 9 * channels)
    mix_rows = jnp.einsum("bhwc,bhwd->cd", gated_act, cotangent, preferred_element_type=jnp.float32)
    grad_term = jnp.concatenate([kernel_rows, mix_rows], axis=1)
    grad_rows = lax.psum_scatter(grad_term, "mp", scatter_dimension=0, tiled=True)
    grad_rows = lax.psum(grad_rows, "dp")
    grad_control = grad_rows[:, : 9 * channels].reshape(grad_rows.shape[0], 3, 3, channels)
    grad_mix = grad_rows[:, 9 * channels :]
    return (output, grad_control, grad_mix, grad_table)


def solution(mesh):
    in_specs = (
        P(("groups", "dp"), "mp", None, None),
        P(("groups", "dp"), "mp", None),
        P(("groups", "dp")),
        P(),
        P(),
        P("mp", None, None, None),
        P("mp", None, None, None),
        P("mp", None),
        P(("groups", "dp"), "mp", None, None),
    )
    out_specs = (
        P(("groups", "dp"), "mp", None, None),
        P(("groups", "mp"), None, None, None),
        P(("groups", "mp"), None),
        P("groups", None),
    )
    return jax.shard_map(
        per_device, mesh=mesh, in_specs=in_specs, out_specs=out_specs, check_vma=False
    )
```

profile of v0, /device:TPU:0, one launch (start us, length us, event | category | flops | bytes accessed | tf_op | source)
XLA Modules:
  0.0 456.9 jit_solution(16254729280796380880)
XLA Ops:
  7.2 0.7 all-gather.5.cloned.1.call-update
  8.0 3.5 fusion.27
  11.5 0.1 pad_maximum_fusion.2
  11.6 1.8 copy-done.6
  13.5 4.9 %collective-permute-start = (bf16[2,3,1,128,320]{3,4,2,1,0:T(8,128)(2,1)S(1)}, bf16[2,3,1,128,320]{3,4,2,1,0:T(8,128)(2,1)S(1)}, u32[]{:S(2)}, u32[]{:S(2)}) collective-permute-start(bf16[2,3,1,128,320]{3,4,2,1,0:T(8,128)(2,1)S(1)} %get-tuple-element.14), channel_id=1, source_target_pairs={{0,2},{2,4},{4,6},{6,8},{8,10},{10,12},{12,14},{1,3},{3,5},{5,7},{... | collective-permute-start | bytes 1474568 | tf_op jit(solution)/shard_map/ppermute | solution.py:16
  18.3 1.3 collective-permute-start.1
  19.7 0.0 reduce-scatter.4.cloned.1.call-start
  19.7 49.6 %all_gather.12 = bf16[320,320]{1,0:T(8,128)(2,1)S(1)} all-gather(bf16[40,320]{1,0:T(8,128)(2,1)S(1)} %copy-done.13), channel_id=1, replica_groups=mesh['groups'=2,'mp'=8,'dp'=2] {'mp'}, dimensions={0}, use_global_device_ids=true | all-gather | bytes 230400 | tf_op jit(solution)/shard_map/all_gather | solution.py:94
  69.4 0.2 multiply_cosine_fusion
  69.6 0.3 fusion.163
  69.9 18.2 %select_maximum_fusion = bf16[2,3,18,130,320]{3,4,2,1,0:T(8,128)(2,1)S(1)} fusion(bf16[2,3,1,128,320]{3,4,2,1,0:T(8,128)(2,1)S(1)} %collective-permute-done.1, bf16[2,3,1,128,320]{3,4,2,1,0:T(8,128)(2,1)S(1)} %collective-permute-done, bf16[1,3,16,128,320]{3,4,2,1,0:T(8,128)(2,1)} %copy-done.6, bf16[1,3,16,128,320]{3,4,2,1,0:T(8,128)(2,1)} %bitcast.302), kind=kLoop, calls=%fused_computation.5 | loop fusion | flops 67392000 | bytes 17832960 | tf_op jit(solution)/shard_map/concatenate | solution.py:14
  88.1 6.6 %slice_bitcast_fusion.1 = (bf16[3,18,130,320]{2,3,1,0:T(8,128)(2,1)}, bf16[3,18,130,320]{2,3,1,0:T(8,128)(2,1)}) fusion(bf16[2,3,18,130,320]{3,4,2,1,0:T(8,128)(2,1)S(1)} %select_maximum_fusion), kind=kLoop, calls=%fused_computation.17 | loop fusion | bytes 17971200 | tf_op jit(solution)/shard_map/squeeze | solution.py:84
  94.7 9.1 %fusion.64 = f32[3,16,128,320]{2,3,1,0:T(8,128)} fusion(bf16[3,18,130,320]{2,3,1,0:T(8,128)(2,1)} %get-tuple-element.13, bf16[320,3,3,320]{3,0,2,1:T(8,128)(2,1)} %all-gather.5.cloned.1.call-done), kind=kOutput, calls=%fused_computation.79 | convolution fusion | flops 1258291200 | bytes 12042240 | tf_op jit(solution)/shard_map/bhwc,cd->bhwd/dot_general | solution.py:39
  103.8 5.3 %fusion.68 = f32[3,16,128,320]{2,3,1,0:T(8,128)} fusion(bf16[3,18,130,320]{2,3,1,0:T(8,128)(2,1)S(1)} %copy-done.2, bf16[320,3,3,320]{3,0,2,1:T(8,128)(2,1)S(1)} %copy-done.9), kind=kOutput, calls=%fused_computation.83 | convolution fusion | flops 1258291200 | bytes 12042240 | tf_op jit(solution)/shard_map/bhwc,cd->bhwd/dot_general | solution.py:39
  109.1 5.5 %fusion.72 = f32[3,16,128,320]{2,3,1,0:T(8,128)} fusion(bf16[3,18,130,320]{2,3,1,0:T(8,128)(2,1)S(1)} %copy-done.2, bf16[320,3,3,320]{3,0,2,1:T(8,128)(2,1)S(1)} %copy-done.9), kind=kOutput, calls=%fused_computation.87 | convolution fusion | flops 1258291200 | bytes 12042240 | tf_op jit(solution)/shard_map/bhwc,cd->bhwd/dot_general | solution.py:39
  114.6 5.5 %fusion.76 = f32[3,16,128,320]{2,3,1,0:T(8,128)} fusion(bf16[3,18,130,320]{2,3,1,0:T(8,128)(2,1)S(1)} %copy-done.2, bf16[320,3,3,320]{3,0,2,1:T(8,128)(2,1)S(1)} %copy-done.9), kind=kOutput, calls=%fused_computation.91 | convolution fusion | flops 1258291200 | bytes 12042240 | tf_op jit(solution)/shard_map/bhwc,cd->bhwd/dot_general | solution.py:39
  120.2 5.3 %fusion.80 = f32[3,16,128,320]{2,3,1,0:T(8,128)} fusion(bf16[3,18,130,320]{2,3,1,0:T(8,128)(2,1)S(1)} %copy-done.2, bf16[320,3,3,320]{3,0,2,1:T(8,128)(2,1)S(1)} %copy-done.9), kind=kOutput, calls=%fused_computation.95 | convolution fusion | flops 1258291200 | bytes 12042240 | tf_op jit(solution)/shard_map/bhwc,cd->bhwd/dot_general | solution.py:39
  125.5 5.8 %fusion.84 = f32[3,16,128,320]{2,3,1,0:T(8,128)} fusion(bf16[3,18,130,320]{2,3,1,0:T(8,128)(2,1)S(1)} %copy-done.2, bf16[320,3,3,320]{3,0,2,1:T(8,128)(2,1)S(1)} %copy-done.9), kind=kOutput, calls=%fused_computation.99 | convolution fusion | flops 1258291200 | bytes 12042240 | tf_op jit(solution)/shard_map/bhwc,cd->bhwd/dot_general | solution.py:39
  131.3 5.7 %fusion.88 = f32[3,16,128,320]{2,3,1,0:T(8,128)} fusion(bf16[3,18,130,320]{2,3,1,0:T(8,128)(2,1)S(1)} %copy-done.2, bf16[320,3,3,320]{3,0,2,1:T(8,128)(2,1)S(1)} %copy-done.9), kind=kOutput, calls=%fused_computation.103 | convolution fusion | flops 1258291200 | bytes 12042240 | tf_op jit(solution)/shard_map/bhwc,cd->bhwd/dot_general | solution.py:39
  137.0 5.4 %fusion.92 = f32[3,16,128,320]{2,3,1,0:T(8,128)} fusion(bf16[3,18,130,320]{2,3,1,0:T(8,128)(2,1)S(1)} %copy-done.2, bf16[320,3,3,320]{3,0,2,1:T(8,128)(2,1)S(1)} %copy-done.9), kind=kOutput, calls=%fused_computation.107 | convolution fusion | flops 1258291200 | bytes 12042240 | tf_op jit(solution)/shard_map/bhwc,cd->bhwd/dot_general | solution.py:39
  142.4 28.2 %multiply_convert_fusion.1 = (bf16[3,16,128,320]{2,3,1,0:T(8,128)(2,1)}, f32[3,16,128,320]{2,3,1,0:T(8,128)}) fusion(f32[3,320]{1,0:T(4,128)S(1)} %fusion.163, bf16[3,18,130,320]{2,3,1,0:T(8,128)(2,1)} %get-tuple-element.13, bf16[320,3,3,320]{3,0,2,1:T(8,128)(2,1)S(1)} %copy-done.9, f32[3,16,128,320]{2,3,1,0:T(8,128)} %fusion.64, ...), kind=kOutput, calls=%fused_computation.29 | convolution fusion | flops 1285816320 | bytes 78895104 | tf_op jit(solution)/shard_map/bhwc,cd->bhwd/dot_general | solution.py:39
  170.6 7.3 %multiply_convert_fusion = bf16[3,16,128,320]{2,3,1,0:T(8,128)(2,1)S(1)} fusion(f32[3,16,128,320]{2,3,1,0:T(8,128)} %get-tuple-element.21, bf16[3,16,128,320]{2,3,1,0:T(8,128)(2,1)} %param.17, bf16[320,320]{1,0:T(8,128)(2,1)S(1)} %all_gather.12), kind=kOutput, calls=%fused_computation.27 | convolution fusion | flops 1275985920 | bytes 15933440 | tf_op jit(solution)/shard_map/bhwd,cd->bhwc/dot_general | solution.py:100
  178.0 5.7 %fusion.101 = f32[320,9,320]{0,2,1:T(8,128)S(1)} fusion(bf16[3,16,128,320]{2,3,1,0:T(8,128)(2,1)S(1)} %multiply_convert_fusion, bf16[3,18,130,320]{2,3,1,0:T(8,128)(2,1)} %get-tuple-element.13), kind=kOutput, calls=%fused_computation.110 | convolution fusion | flops 1258291200 | bytes 8355840 | tf_op jit(solution)/shard_map/bhwc,bhwd->cd/dot_general | solution.py:117
  183.7 1.3 collective-permute-start.2
  185.1 1.9 collective-permute-start.3
  187.0 5.5 %fusion.107 = f32[320,9,320]{0,2,1:T(8,128)S(1)} fusion(f32[320,9,320]{0,2,1:T(8,128)S(1)} %fusion.101, bf16[3,16,128,320]{2,3,1,0:T(8,128)(2,1)S(1)} %multiply_convert_fusion, bf16[3,18,130,320]{2,3,1,0:T(8,128)(2,1)} %get-tuple-element.13), kind=kOutput, calls=%fused_computation.112 | convolution fusion | flops 1258291200 | bytes 8355840 | tf_op jit(solution)/shard_map/bhwc,bhwd->cd/dot_general | solution.py:117
  192.5 2.3 fusion.113
  194.8 2.2 fusion.119
  197.0 2.3 fusion.125
  199.3 2.3 fusion.131
  201.6 2.2 fusion.137
  203.8 2.5 fusion.143
  206.3 2.3 fusion.149
  208.6 2.2 copy-done.10
  210.8 5.6 %copy.38 = f32[320,2880]{1,0:T(8,128)} copy(f32[320,2880]{0,1:T(8,128)} %bitcast.304) | data formatting | bytes 7372800 | tf_op jit(solution)/shard_map/reshape | solution.py:124
  216.4 7.6 %fusion.156 = f32[3,16,128,320]{2,3,1,0:T(8,128)} fusion(bf16[3,16,128,320]{2,3,1,0:T(8,128)(2,1)} %get-tuple-element.20, bf16[320,320]{1,0:T(8,128)(2,1)S(1)} %all_gather.12), kind=kOutput, calls=%fused_computation.151 | convolution fusion | flops 1258291200 | bytes 12001280 | tf_op jit(solution)/shard_map/bhwc,cd->bhwd/dot_general | solution.py:98
  224.0 2.2 convolution_bitcast_fusion
  226.2 2.3 pad_maximum_fusion
  228.6 0.0 all-reduce.5.cloned.1.call-start
  228.7 9.0 %fusion.42 = f32[3,16,128,320]{2,3,1,0:T(8,128)} fusion(bf16[3,18,130,320]{2,3,1,0:T(8,128)(2,1)} %get-tuple-element.12, bf16[320,3,3,320]{3,0,2,1:T(8,128)(2,1)} %all-gather.3.cloned.1.call-done), kind=kOutput, calls=%fused_computation.57 | convolution fusion | flops 1258291200 | bytes 12042240 | tf_op jit(solution)/shard_map/bhwc,cd->bhwd/dot_general | solution.py:39
  237.7 7.5 %fusion.44 = f32[3,16,128,320]{2,3,1,0:T(8,128)} fusion(bf16[3,18,130,320]{2,3,1,0:T(8,128)(2,1)} %get-tuple-element.12, bf16[320,3,3,320]{3,0,2,1:T(8,128)(2,1)S(1)} %copy-done.11), kind=kOutput, calls=%fused_computation.59 | convolution fusion | flops 1258291200 | bytes 12042240 | tf_op jit(solution)/shard_map/bhwc,cd->bhwd/dot_general | solution.py:39
  245.2 5.5 %fusion.46 = f32[3,16,128,320]{2,3,1,0:T(8,128)} fusion(bf16[3,18,130,320]{2,3,1,0:T(8,128)(2,1)S(1)} %bitcast.299, bf16[320,3,3,320]{3,0,2,1:T(8,128)(2,1)S(1)} %copy-done.11), kind=kOutput, calls=%fused_computation.61 | convolution fusion | flops 1258291200 | bytes 12042240 | tf_op jit(solution)/shard_map/bhwc,cd->bhwd/dot_general | solution.py:39
  250.7 5.6 %fusion.48 = f32[3,16,128,320]{2,3,1,0:T(8,128)} fusion(bf16[3,18,130,320]{2,3,1,0:T(8,128)(2,1)S(1)} %bitcast.299, bf16[320,3,3,320]{3,0,2,1:T(8,128)(2,1)S(1)} %copy-done.11), kind=kOutput, calls=%fused_computation.63 | convolution fusion | flops 1258291200 | bytes 12042240 | tf_op jit(solution)/shard_map/bhwc,cd->bhwd/dot_general | solution.py:39
  256.3 5.3 %fusion.50 = f32[3,16,128,320]{2,3,1,0:T(8,128)} fusion(bf16[3,18,130,320]{2,3,1,0:T(8,128)(2,1)S(1)} %bitcast.299, bf16[320,3,3,320]{3,0,2,1:T(8,128)(2,1)S(1)} %copy-done.11), kind=kOutput, calls=%fused_computation.65 | convolution fusion | flops 1258291200 | bytes 12042240 | tf_op jit(solution)/shard_map/bhwc,cd->bhwd/dot_general | solution.py:39
  261.6 6.0 %fusion.52 = f32[3,16,128,320]{2,3,1,0:T(8,128)} fusion(bf16[3,18,130,320]{2,3,1,0:T(8,128)(2,1)S(1)} %bitcast.299, bf16[320,3,3,320]{3,0,2,1:T(8,128)(2,1)S(1)} %copy-done.11), kind=kOutput, calls=%fused_computation.67 | convolution fusion | flops 1258291200 | bytes 12042240 | tf_op jit(solution)/shard_map/bhwc,cd->bhwd/dot_general | solution.py:39
  267.6 5.6 %fusion.54 = f32[3,16,128,320]{2,3,1,0:T(8,128)} fusion(bf16[3,18,130,320]{2,3,1,0:T(8,128)(2,1)S(1)} %bitcast.299, bf16[320,3,3,320]{3,0,2,1:T(8,128)(2,1)S(1)} %copy-done.11), kind=kOutput, calls=%fused_computation.69 | convolution fusion | flops 1258291200 | bytes 12042240 | tf_op jit(solution)/shard_map/bhwc,cd->bhwd/dot_general | solution.py:39
  273.2 5.3 %fusion.56 = f32[3,16,128,320]{2,3,1,0:T(8,128)} fusion(bf16[3,18,130,320]{2,3,1,0:T(8,128)(2,1)S(1)} %bitcast.299, bf16[320,3,3,320]{3,0,2,1:T(8,128)(2,1)S(1)} %copy-done.11), kind=kOutput, calls=%fused_computation.71 | convolution fusion | flops 1258291200 | bytes 12042240 | tf_op jit(solution)/shard_map/bhwc,cd->bhwd/dot_general | solution.py:39
  278.5 28.6 %add_convert_fusion = bf16[3,16,128,320]{2,3,1,0:T(8,128)(2,1)} fusion(f32[3,16,128,320]{2,3,1,0:T(8,128)} %fusion.156, f32[3,16,128,320]{2,3,1,0:T(8,128)} %fusion.42, f32[3,16,128,320]{2,3,1,0:T(8,128)} %fusion.44, f32[3,16,128,320]{2,3,1,0:T(8,128)} %fusion.46, f32[3,16,128,320]{2,3,1,0:T(8,128)} %fusion.48, f32[3,16,128,320]{2,3,1,0:T(8,128)} %fusion.50, ...), kind=kOutput, calls=%fused_computation.28 | convolution fusion | flops 1287782400 | bytes 78892800 | tf_op jit(solution)/shard_map/bhwc,cd->bhwd/dot_general | solution.py:39
  307.2 7.6 %fusion.158 = f32[3,16,128,320]{2,3,1,0:T(8,128)} fusion(bf16[3,16,128,320]{2,3,1,0:T(8,128)(2,1)} %copy-done.3, bf16[320,3,3,320]{3,0,2,1:T(8,128)(2,1)S(1)} %copy-done.9), kind=kOutput, calls=%fused_computation.153 | convolution fusion | flops 1258291200 | bytes 12042240 | tf_op jit(solution)/shard_map/bhwd,cd->bhwc/dot_general | solution.py:54
  314.8 5.3 %fusion.19 = f32[3,16,128,320]{2,3,1,0:T(8,128)} fusion(bf16[3,1,128,320]{2,3,1,0:T(8,128)(2,1)S(1)} %collective-permute-done.3, bf16[3,16,128,320]{2,3,1,0:T(8,128)(2,1)S(1)} %copy-done.4, bf16[320,3,3,320]{3,0,2,1:T(8,128)(2,1)S(1)} %copy-done.9), kind=kOutput, calls=%fused_computation.33 | convolution fusion | flops 1266647040 | bytes 12288000 | tf_op jit(solution)/shard_map/bhwd,cd->bhwc/dot_general | solution.py:54
  320.1 5.3 %fusion.23 = f32[3,16,128,320]{2,3,1,0:T(8,128)} fusion(bf16[3,16,128,320]{2,3,1,0:T(8,128)(2,1)S(1)} %copy-done.4, bf16[3,1,128,320]{2,3,1,0:T(8,128)(2,1)S(1)} %collective-permute-done.2, bf16[320,3,3,320]{3,0,2,1:T(8,128)(2,1)S(1)} %copy-done.9), kind=kOutput, calls=%fused_computation.37 | convolution fusion | flops 1266647040 | bytes 12288000 | tf_op jit(solution)/shard_map/bhwd,cd->bhwc/dot_general | solution.py:54
  325.4 6.3 %fusion.9 = bf16[3,18,130,320]{2,3,1,0:T(8,128)(2,1)S(1)} fusion(bf16[3,1,128,320]{2,3,1,0:T(8,128)(2,1)S(1)} %collective-permute-done.3, bf16[3,16,128,320]{2,3,1,0:T(8,128)(2,1)S(1)} %copy-done.4, bf16[3,1,128,320]{2,3,1,0:T(8,128)(2,1)S(1)} %collective-permute-done.2), kind=kLoop, calls=%fused_computation.15 | loop fusion | flops 26956800 | bytes 8916480 | tf_op jit(solution)/shard_map/concatenate | solution.py:14
  331.8 5.5 %fusion.30 = f32[3,16,128,320]{2,3,1,0:T(8,128)} fusion(bf16[3,18,130,320]{2,3,1,0:T(8,128)(2,1)S(1)} %fusion.9, bf16[320,3,3,320]{3,0,2,1:T(8,128)(2,1)S(1)} %copy-done.9), kind=kOutput, calls=%fused_computation.45 | convolution fusion | flops 1258291200 | bytes 12042240 | tf_op jit(solution)/shard_map/bhwd,cd->bhwc/dot_general | solution.py:54
  337.3 5.3 %fusion.32 = f32[3,16,128,320]{2,3,1,0:T(8,128)} fusion(bf16[3,18,130,320]{2,3,1,0:T(8,128)(2,1)S(1)} %fusion.9, bf16[320,3,3,320]{3,0,2,1:T(8,128)(2,1)S(1)} %copy-done.9), kind=kOutput, calls=%fused_computation.47 | convolution fusion | flops 1258291200 | bytes 12042240 | tf_op jit(solution)/shard_map/bhwd,cd->bhwc/dot_general | solution.py:54
  342.7 5.5 %fusion.34 = f32[3,16,128,320]{2,3,1,0:T(8,128)} fusion(bf16[3,18,130,320]{2,3,1,0:T(8,128)(2,1)S(1)} %fusion.9, bf16[320,3,3,320]{3,0,2,1:T(8,128)(2,1)S(1)} %copy-done.9), kind=kOutput, calls=%fused_computation.49 | convolution fusion | flops 1258291200 | bytes 12042240 | tf_op jit(solution)/shard_map/bhwd,cd->bhwc/dot_general | solution.py:54
  348.2 5.4 %fusion.36 = f32[3,16,128,320]{2,3,1,0:T(8,128)} fusion(bf16[3,18,130,320]{2,3,1,0:T(8,128)(2,1)S(1)} %fusion.9, bf16[320,3,3,320]{3,0,2,1:T(8,128)(2,1)S(1)} %copy-done.9), kind=kOutput, calls=%fused_computation.51 | convolution fusion | flops 1258291200 | bytes 12042240 | tf_op jit(solution)/shard_map/bhwd,cd->bhwc/dot_general | solution.py:54
  353.6 5.5 %fusion.38 = f32[3,16,128,320]{2,3,1,0:T(8,128)} fusion(bf16[3,18,130,320]{2,3,1,0:T(8,128)(2,1)S(1)} %fusion.9, bf16[320,3,3,320]{3,0,2,1:T(8,128)(2,1)S(1)} %copy-done.9), kind=kOutput, calls=%fused_computation.53 | convolution fusion | flops 1258291200 | bytes 12042240 | tf_op jit(solution)/shard_map/bhwd,cd->bhwc/dot_general | solution.py:54
  359.0 5.3 %fusion.28 = f32[3,16,128,320]{2,3,1,0:T(8,128)} fusion(bf16[3,18,130,320]{2,3,1,0:T(8,128)(2,1)S(1)} %fusion.9, bf16[320,3,3,320]{3,0,2,1:T(8,128)(2,1)S(1)} %copy-done.9), kind=kOutput, calls=%fused_computation.43 | convolution fusion | flops 1258291200 | bytes 12042240 | tf_op jit(solution)/shard_map/bhwd,cd->bhwc/dot_general | solution.py:54
  364.4 24.3 %fusion.152 = f32[16,320]{1,0:T(8,128)S(1)} fusion(f32[3,16,128,320]{2,3,1,0:T(8,128)} %fusion.28, f32[3,16,128,320]{2,3,1,0:T(8,128)} %fusion.23, f32[3,16,128,320]{2,3,1,0:T(8,128)} %fusion.30, f32[3,16,128,320]{2,3,1,0:T(8,128)} %fusion.32, f32[3,16,128,320]{2,3,1,0:T(8,128)} %fusion.158, f32[3,16,128,320]{2,3,1,0:T(8,128)} %fusion.34, ...), kind=kOutput, calls=%fused_computation.128 | convolution fusion | flops 393314304 | bytes 70823936 | tf_op jit(solution)/shard_map/bhwr,bhwc->rc/dot_general | solution.py:109
  388.7 57.6 %psum.15 = f32[16,320]{1,0:T(8,128)} all-reduce(f32[16,320]{1,0:T(8,128)S(1)} %fusion.152), channel_id=1, replica_groups=mesh['groups'=2,'mp'=8,'dp'=2] {'mp','dp'}, use_global_device_ids=true, to_apply=%region_2.3 | all-reduce | flops 5120 | bytes 40960 | tf_op jit(solution)/shard_map/psum | solution.py:112
  446.3 1.1 slice.270
  447.4 0.4 reshape.23
  447.8 0.8 copy.48
  448.6 1.5 slice.271
  (60 shorter events, 0.4 us)
Async XLA Ops:
  7.2 62.4 %copy-start = (bf16[1280,320]{0,1:T(8,128)(2,1)S(1)}, bf16[1280,320]{0,1:T(8,128)(2,1)}, u32[]{:S(2)}) copy-start(bf16[1280,320]{0,1:T(8,128)(2,1)} %param.13) | copy-start | bytes 2457604
  7.2 87.5 %all-gather.5.cloned.1.call-start = ((), (), s32[]{:S(2)}) async-start(), calls=%async_computation.2 | async-start | bytes 2488320 | tf_op jit(solution)/shard_map/all_gather | solution.py:93
  7.9 11.8 %copy-start.13 = (bf16[40,320]{1,0:T(8,128)(2,1)S(1)}, bf16[40,320]{1,0:T(8,128)(2,1)}, u32[]{:S(2)}) copy-start(bf16[40,320]{1,0:T(8,128)(2,1)} %param.16) | copy-start | bytes 76804
  7.9 61.5 %copy-start.15 = (s32[3]{0:T(128)S(1)}, s32[3]{0:T(128)}, u32[]{:S(2)}) copy-start(s32[3]{0:T(128)} %param.11) | copy-start | bytes 40
  7.9 220.7 %all-gather.3.cloned.1.call-start = ((), (), s32[]{:S(2)}) async-start(), calls=%async_computation.1 | async-start | bytes 2488320 | tf_op jit(solution)/shard_map/all_gather | solution.py:90
  8.0 3.6 copy-start.5
  11.5 1.9 copy-start.6
  13.5 56.4 %collective-permute-start = (bf16[2,3,1,128,320]{3,4,2,1,0:T(8,128)(2,1)S(1)}, bf16[2,3,1,128,320]{3,4,2,1,0:T(8,128)(2,1)S(1)}, u32[]{:S(2)}, u32[]{:S(2)}) collective-permute-start(bf16[2,3,1,128,320]{3,4,2,1,0:T(8,128)(2,1)S(1)} %get-tuple-element.14), channel_id=1, source_target_pairs={{0,2},{2,4},{4,6},{6,8},{8,10},{10,12},{12,14},{1,3},{3,5},{5,7},{... | collective-permute-start | bytes 1474568 | tf_op jit(solution)/shard_map/ppermute | solution.py:16
  18.3 51.5 %collective-permute-start.1 = (bf16[2,3,1,128,320]{3,4,2,1,0:T(8,128)(2,1)S(1)}, bf16[2,3,1,128,320]{3,4,2,1,0:T(8,128)(2,1)S(1)}, u32[]{:S(2)}, u32[]{:S(2)}) collective-permute-start(bf16[2,3,1,128,320]{3,4,2,1,0:T(8,128)(2,1)S(1)} %get-tuple-element.15), channel_id=1, source_target_pairs={{2,0},{4,2},{6,4},{8,6},{10,8},{12,10},{14,12},{3,1},{5,3},{7,5},{... | collective-permute-start | bytes 1474568 | tf_op jit(solution)/shard_map/ppermute | solution.py:18
  19.7 344.7 %reduce-scatter.4.cloned.1.call-start = ((), (), s32[]{:S(2)}) async-start(), calls=%async_computation.4 | async-start | bytes 4608000
  94.7 9.1 %copy-start.2 = (bf16[3,18,130,320]{2,3,1,0:T(8,128)(2,1)S(1)}, bf16[3,18,130,320]{2,3,1,0:T(8,128)(2,1)}, u32[]{:S(2)}) copy-start(bf16[3,18,130,320]{2,3,1,0:T(8,128)(2,1)} %get-tuple-element.13) | copy-start | bytes 13478404
  94.7 9.1 %copy-start.9 = (bf16[320,3,3,320]{3,0,2,1:T(8,128)(2,1)S(1)}, bf16[320,3,3,320]{3,0,2,1:T(8,128)(2,1)}, u32[]{:S(2)}) copy-start(bf16[320,3,3,320]{3,0,2,1:T(8,128)(2,1)} %all-gather.5.cloned.1.call-done) | copy-start | bytes 5529604
  177.9 28.4 %copy-start.3 = (bf16[3,16,128,320]{2,3,1,0:T(8,128)(2,1)}, bf16[3,16,128,320]{2,3,1,0:T(8,128)(2,1)S(1)}, u32[]{:S(2)}) copy-start(bf16[3,16,128,320]{2,3,1,0:T(8,128)(2,1)S(1)} %multiply_convert_fusion) | copy-start | bytes 11796484
  178.0 14.5 %slice-start.3 = ((s8[8847360]{0:T(1024)(128)(4,1)}), s8[4194304]{0:T(1024)(128)(4,1)S(1)}, s32[]{:S(2)}) async-start(s8[8847360]{0:T(1024)(128)(4,1)} %bitcast.300), calls=%async_computation.8 | async-start | bytes 8388608
  178.0 14.5 %slice-start.4 = ((s8[8847360]{0:T(1024)(128)(4,1)}), s8[4194304]{0:T(1024)(128)(4,1)S(1)}, s32[]{:S(2)}) async-start(s8[8847360]{0:T(1024)(128)(4,1)} %bitcast.300), calls=%async_computation.9 | async-start | bytes 8388608
  183.7 136.3 %collective-permute-start.2 = (bf16[3,1,128,320]{2,3,1,0:T(8,128)(2,1)S(1)}, bf16[3,1,128,320]{2,3,1,0:T(8,128)(2,1)S(1)}, u32[]{:S(2)}, u32[]{:S(2)}) collective-permute-start(bf16[3,1,128,320]{2,3,1,0:T(8,128)(2,1)S(1)} %get-tuple-element.16), channel_id=1, source_target_pairs={{0,2},{2,4},{4,6},{6,8},{8,10},{10,12},{12,14},{1,3},{3,5},{5,7},{... | collective-permute-start | bytes 737288 | tf_op jit(solution)/shard_map/ppermute | solution.py:16
  185.1 7.5 %slice-start.5 = ((s8[8847360]{0:T(1024)(128)(4,1)}), s8[458752]{0:T(1024)(128)(4,1)S(1)}, s32[]{:S(2)}) async-start(s8[8847360]{0:T(1024)(128)(4,1)} %bitcast.300), calls=%async_computation.10 | async-start | bytes 917504
  185.1 129.7 %collective-permute-start.3 = (bf16[3,1,128,320]{2,3,1,0:T(8,128)(2,1)S(1)}, bf16[3,1,128,320]{2,3,1,0:T(8,128)(2,1)S(1)}, u32[]{:S(2)}, u32[]{:S(2)}) collective-permute-start(bf16[3,1,128,320]{2,3,1,0:T(8,128)(2,1)S(1)} %get-tuple-element.17), channel_id=1, source_target_pairs={{2,0},{4,2},{6,4},{8,6},{10,8},{12,10},{14,12},{3,1},{5,3},{7,5},{... | collective-permute-start | bytes 737288 | tf_op jit(solution)/shard_map/ppermute | solution.py:18
  208.6 2.2 copy-start.10
  216.4 7.6 %copy-start.7 = (bf16[3,16,128,320]{2,3,1,0:T(8,128)(2,1)S(1)}, bf16[3,16,128,320]{2,3,1,0:T(8,128)(2,1)}, u32[]{:S(2)}) copy-start(bf16[3,16,128,320]{2,3,1,0:T(8,128)(2,1)} %get-tuple-element.20) | copy-start | bytes 11796484
  216.4 7.6 %copy-start.14 = (bf16[3,16,128,320]{2,3,1,0:T(8,128)(2,1)S(1)}, bf16[3,16,128,320]{2,3,1,0:T(8,128)(2,1)}, u32[]{:S(2)}) copy-start(bf16[3,16,128,320]{2,3,1,0:T(8,128)(2,1)} %param.17) | copy-start | bytes 11796484
  224.0 2.2 copy-start.8
  228.6 217.7 %all-reduce.5.cloned.1.call-start = ((), (), s32[]{:S(2)}) async-start(), calls=%async_computation.3 | async-start | bytes 1024000 | tf_op jit(solution)/shard_map/psum | solution.py:128
  228.7 9.0 %copy-start.11 = (bf16[320,3,3,320]{3,0,2,1:T(8,128)(2,1)S(1)}, bf16[320,3,3,320]{3,0,2,1:T(8,128)(2,1)}, u32[]{:S(2)}) copy-start(bf16[320,3,3,320]{3,0,2,1:T(8,128)(2,1)} %all-gather.3.cloned.1.call-done) | copy-start | bytes 5529604
  228.7 16.5 %slice-start = ((s8[8847360]{0:T(1024)(128)(4,1)}), s8[4194304]{0:T(1024)(128)(4,1)S(1)}, s32[]{:S(2)}) async-start(s8[8847360]{0:T(1024)(128)(4,1)} %bitcast.298), calls=%async_computation.5 | async-start | bytes 8388608
  228.7 16.5 %slice-start.1 = ((s8[8847360]{0:T(1024)(128)(4,1)}), s8[4194304]{0:T(1024)(128)(4,1)S(1)}, s32[]{:S(2)}) async-start(s8[8847360]{0:T(1024)(128)(4,1)} %bitcast.298), calls=%async_computation.6 | async-start | bytes 8388608
  237.7 7.5 %slice-start.2 = ((s8[8847360]{0:T(1024)(128)(4,1)}), s8[458752]{0:T(1024)(128)(4,1)S(1)}, s32[]{:S(2)}) async-start(s8[8847360]{0:T(1024)(128)(4,1)} %bitcast.298), calls=%async_computation.7 | async-start | bytes 917504
  307.2 7.6 %copy-start.4 = (bf16[3,16,128,320]{2,3,1,0:T(8,128)(2,1)S(1)}, bf16[3,16,128,320]{2,3,1,0:T(8,128)(2,1)}, u32[]{:S(2)}) copy-start(bf16[3,16,128,320]{2,3,1,0:T(8,128)(2,1)} %copy-done.3) | copy-start | bytes 11796484
  359.0 5.4 %copy-start.12 = (s32[3,16,128]{2,1,0:T(8,128)S(1)}, s32[3,16,128]{2,1,0:T(8,128)}, u32[]{:S(2)}) copy-start(s32[3,16,128]{2,1,0:T(8,128)} %param.10) | copy-start | bytes 73732
  364.4 85.8 %copy-start.1 = (bf16[1280,320]{0,1:T(8,128)(2,1)S(1)}, bf16[1280,320]{0,1:T(8,128)(2,1)}, u32[]{:S(2)}) copy-start(bf16[1280,320]{0,1:T(8,128)(2,1)} %param.13) | copy-start | bytes 2457604
Sparse Core Ops, SparseCore 0:
  10.2 66.9 all-gather.4
  79.4 49.2 all-gather.2
  228.7 87.1 reduce-scatter.3
  364.5 20.1 all-reduce.4
where the time goes:
time: 461 us; the launch traced here: 457 us
  matrix products  278 us (60%)
  blocking collectives  107 us (23%)
  other arithmetic  27.1 us (6%)
  local copies, waits for them, and re-layouts  20.2 us (4%)
  between operations  14.4 us (3%)
  starting transfers between devices  9.53 us (2%)
    dot_general x18, matrix products, forward_taps(): jnp.einsum('bhwc,cd->bhwd', frame[:, tap_row:tap_row + row_count, tap_col...  154 us
    psum x1, blocking collectives, per_device(): grad_table = lax.psum(table_local, ('mp', 'dp'))  57.6 us
    dot_general x9, matrix products, backward_taps(): jnp.einsum('bhwd,cd->bhwc', frame[:, 2 - tap_row:2 - tap_row + row_count,...  50.8 us
    all_gather x1, blocking collectives, per_device(): lax.all_gather(mix_weight, 'mp', axis=0, tiled=True)  49.6 us
    dot_general x9, matrix products, per_device(): jnp.einsum('bhwc,bhwd->cd', control_frame[:, tap_row:tap_row + row_count,...  27.3 us
    concatenate x2, other arithmetic, with_halo(): jnp.concatenate([lax.ppermute(tail, axis, [(i, (i + 1) % count) for i in...  24.5 us
    dot_general x1, matrix products, per_device(): jnp.einsum('bhwr,bhwc->rc', onehot.astype(jnp.float32), back_in, precisio...  24.3 us
  transfers between devices with their start and end apart: 8, of which 0 were waited for; matrix products, arithmetic and copies ran while one was open for 69% of the time, Pallas kernels for 0%

commit v1 on v0

--- a/solution.py
+++ b/solution.py
@@ -109,7 +109,9 @@
     table_local = jnp.einsum(
         "bhwr,bhwc->rc", onehot.astype(jnp.float32), back_in, precision=lax.Precision.HIGHEST
     )
-    grad_table = lax.psum(table_local, ("mp", "dp"))
+    grad_table = table_local
+    for name in ("dp", "mp"):
+        grad_table = lax.psum(grad_table, name)
     pieces = []
     for tap_row in range(3):
         for tap_col in range(3):

time: 461 us -> 444 us (0.963)
  blocking collectives: 107 us -> 90.4 us
    psum x1 -> x2, blocking collectives: 57.6 us -> 40.8 us  [per_device(): grad_table = lax.psum(grad_table, name)]
  transfers between devices with their start and end apart: 8 -> 8, of which waited for: 0 -> 0; matrix products, arithmetic and copies ran while one was open for 69% -> 72% of each run, Pallas kernels for 0% -> 0%
where the time goes in v1:
time: 444 us; the launch traced here: 440 us
  matrix products  278 us (63%)
  blocking collectives  90.4 us (20%)
  other arithmetic  27.1 us (6%)
  local copies, waits for them, and re-layouts  20.3 us (5%)
  between operations  14.5 us (3%)
  starting transfers between devices  9.53 us (2%)
    dot_general x18, matrix products, forward_taps(): jnp.einsum('bhwc,cd->bhwd', frame[:, tap_row:tap_row + row_count, tap_col...  154 us
    dot_general x9, matrix products, backward_taps(): jnp.einsum('bhwd,cd->bhwc', frame[:, 2 - tap_row:2 - tap_row + row_count,...  50.8 us
    all_gather x1, blocking collectives, per_device(): lax.all_gather(mix_weight, 'mp', axis=0, tiled=True)  49.6 us
    psum x2, blocking collectives, per_device(): grad_table = lax.psum(grad_table, name)  40.8 us
    dot_general x9, matrix products, per_device(): jnp.einsum('bhwc,bhwd->cd', control_frame[:, tap_row:tap_row + row_count,...  27.3 us
    concatenate x2, other arithmetic, with_halo(): jnp.concatenate([lax.ppermute(tail, axis, [(i, (i + 1) % count) for i in...  24.5 us
    dot_general x1, matrix products, per_device(): jnp.einsum('bhwr,bhwc->rc', onehot.astype(jnp.float32), back_in, precisio...  24.3 us
  transfers between devices with their start and end apart: 8, of which 0 were waited for; matrix products, arithmetic and copies ran while one was open for 72% of the time, Pallas kernels for 0%

profile of v1, /device:TPU:0, one launch (start us, length us, event | category | flops | bytes accessed | tf_op | source)
XLA Modules:
  0.0 440.2 jit_solution(11632140233852733703)
XLA Ops:
  7.2 0.7 all-gather.5.cloned.1.call-update
  8.0 3.5 fusion.27
  11.5 0.1 pad_maximum_fusion.2
  11.6 1.8 copy-done.6
  13.5 4.9 %collective-permute-start = (bf16[2,3,1,128,320]{3,4,2,1,0:T(8,128)(2,1)S(1)}, bf16[2,3,1,128,320]{3,4,2,1,0:T(8,128)(2,1)S(1)}, u32[]{:S(2)}, u32[]{:S(2)}) collective-permute-start(bf16[2,3,1,128,320]{3,4,2,1,0:T(8,128)(2,1)S(1)} %get-tuple-element.14), channel_id=1, source_target_pairs={{0,2},{2,4},{4,6},{6,8},{8,10},{10,12},{12,14},{1,3},{3,5},{5,7},{... | collective-permute-start | bytes 1474568 | tf_op jit(solution)/shard_map/ppermute | solution.py:16
  18.3 1.3 collective-permute-start.1
  19.7 0.0 reduce-scatter.4.cloned.1.call-start
  19.7 49.6 %all_gather.12 = bf16[320,320]{1,0:T(8,128)(2,1)S(1)} all-gather(bf16[40,320]{1,0:T(8,128)(2,1)S(1)} %copy-done.13), channel_id=1, replica_groups=mesh['groups'=2,'mp'=8,'dp'=2] {'mp'}, dimensions={0}, use_global_device_ids=true | all-gather | bytes 230400 | tf_op jit(solution)/shard_map/all_gather | solution.py:94
  69.4 0.2 multiply_cosine_fusion
  69.6 0.3 fusion.163
  69.9 18.2 %select_maximum_fusion = bf16[2,3,18,130,320]{3,4,2,1,0:T(8,128)(2,1)S(1)} fusion(bf16[2,3,1,128,320]{3,4,2,1,0:T(8,128)(2,1)S(1)} %collective-permute-done.1, bf16[2,3,1,128,320]{3,4,2,1,0:T(8,128)(2,1)S(1)} %collective-permute-done, bf16[1,3,16,128,320]{3,4,2,1,0:T(8,128)(2,1)} %copy-done.6, bf16[1,3,16,128,320]{3,4,2,1,0:T(8,128)(2,1)} %bitcast.302), kind=kLoop, calls=%fused_computation.5 | loop fusion | flops 67392000 | bytes 17832960 | tf_op jit(solution)/shard_map/concatenate | solution.py:14
  88.1 6.7 %slice_bitcast_fusion.1 = (bf16[3,18,130,320]{2,3,1,0:T(8,128)(2,1)}, bf16[3,18,130,320]{2,3,1,0:T(8,128)(2,1)}) fusion(bf16[2,3,18,130,320]{3,4,2,1,0:T(8,128)(2,1)S(1)} %select_maximum_fusion), kind=kLoop, calls=%fused_computation.17 | loop fusion | bytes 17971200 | tf_op jit(solution)/shard_map/squeeze | solution.py:84
  94.8 9.1 %fusion.64 = f32[3,16,128,320]{2,3,1,0:T(8,128)} fusion(bf16[3,18,130,320]{2,3,1,0:T(8,128)(2,1)} %get-tuple-element.13, bf16[320,3,3,320]{3,0,2,1:T(8,128)(2,1)} %all-gather.5.cloned.1.call-done), kind=kOutput, calls=%fused_computation.79 | convolution fusion | flops 1258291200 | bytes 12042240 | tf_op jit(solution)/shard_map/bhwc,cd->bhwd/dot_general | solution.py:39
  103.9 5.3 %fusion.68 = f32[3,16,128,320]{2,3,1,0:T(8,128)} fusion(bf16[3,18,130,320]{2,3,1,0:T(8,128)(2,1)S(1)} %copy-done.2, bf16[320,3,3,320]{3,0,2,1:T(8,128)(2,1)S(1)} %copy-done.9), kind=kOutput, calls=%fused_computation.83 | convolution fusion | flops 1258291200 | bytes 12042240 | tf_op jit(solution)/shard_map/bhwc,cd->bhwd/dot_general | solution.py:39
  109.2 5.5 %fusion.72 = f32[3,16,128,320]{2,3,1,0:T(8,128)} fusion(bf16[3,18,130,320]{2,3,1,0:T(8,128)(2,1)S(1)} %copy-done.2, bf16[320,3,3,320]{3,0,2,1:T(8,128)(2,1)S(1)} %copy-done.9), kind=kOutput, calls=%fused_computation.87 | convolution fusion | flops 1258291200 | bytes 12042240 | tf_op jit(solution)/shard_map/bhwc,cd->bhwd/dot_general | solution.py:39
  114.7 5.5 %fusion.76 = f32[3,16,128,320]{2,3,1,0:T(8,128)} fusion(bf16[3,18,130,320]{2,3,1,0:T(8,128)(2,1)S(1)} %copy-done.2, bf16[320,3,3,320]{3,0,2,1:T(8,128)(2,1)S(1)} %copy-done.9), kind=kOutput, calls=%fused_computation.91 | convolution fusion | flops 1258291200 | bytes 12042240 | tf_op jit(solution)/shard_map/bhwc,cd->bhwd/dot_general | solution.py:39
  120.2 5.3 %fusion.80 = f32[3,16,128,320]{2,3,1,0:T(8,128)} fusion(bf16[3,18,130,320]{2,3,1,0:T(8,128)(2,1)S(1)} %copy-done.2, bf16[320,3,3,320]{3,0,2,1:T(8,128)(2,1)S(1)} %copy-done.9), kind=kOutput, calls=%fused_computation.95 | convolution fusion | flops 1258291200 | bytes 12042240 | tf_op jit(solution)/shard_map/bhwc,cd->bhwd/dot_general | solution.py:39
  125.6 5.8 %fusion.84 = f32[3,16,128,320]{2,3,1,0:T(8,128)} fusion(bf16[3,18,130,320]{2,3,1,0:T(8,128)(2,1)S(1)} %copy-done.2, bf16[320,3,3,320]{3,0,2,1:T(8,128)(2,1)S(1)} %copy-done.9), kind=kOutput, calls=%fused_computation.99 | convolution fusion | flops 1258291200 | bytes 12042240 | tf_op jit(solution)/shard_map/bhwc,cd->bhwd/dot_general | solution.py:39
  131.4 5.7 %fusion.88 = f32[3,16,128,320]{2,3,1,0:T(8,128)} fusion(bf16[3,18,130,320]{2,3,1,0:T(8,128)(2,1)S(1)} %copy-done.2, bf16[320,3,3,320]{3,0,2,1:T(8,128)(2,1)S(1)} %copy-done.9), kind=kOutput, calls=%fused_computation.103 | convolution fusion | flops 1258291200 | bytes 12042240 | tf_op jit(solution)/shard_map/bhwc,cd->bhwd/dot_general | solution.py:39
  137.1 5.4 %fusion.92 = f32[3,16,128,320]{2,3,1,0:T(8,128)} fusion(bf16[3,18,130,320]{2,3,1,0:T(8,128)(2,1)S(1)} %copy-done.2, bf16[320,3,3,320]{3,0,2,1:T(8,128)(2,1)S(1)} %copy-done.9), kind=kOutput, calls=%fused_computation.107 | convolution fusion | flops 1258291200 | bytes 12042240 | tf_op jit(solution)/shard_map/bhwc,cd->bhwd/dot_general | solution.py:39
  142.5 28.2 %multiply_convert_fusion.1 = (bf16[3,16,128,320]{2,3,1,0:T(8,128)(2,1)}, f32[3,16,128,320]{2,3,1,0:T(8,128)}) fusion(f32[3,320]{1,0:T(4,128)S(1)} %fusion.163, bf16[3,18,130,320]{2,3,1,0:T(8,128)(2,1)} %get-tuple-element.13, bf16[320,3,3,320]{3,0,2,1:T(8,128)(2,1)S(1)} %copy-done.9, f32[3,16,128,320]{2,3,1,0:T(8,128)} %fusion.64, ...), kind=kOutput, calls=%fused_computation.29 | convolution fusion | flops 1285816320 | bytes 78895104 | tf_op jit(solution)/shard_map/bhwc,cd->bhwd/dot_general | solution.py:39
  170.7 7.3 %multiply_convert_fusion = bf16[3,16,128,320]{2,3,1,0:T(8,128)(2,1)S(1)} fusion(f32[3,16,128,320]{2,3,1,0:T(8,128)} %get-tuple-element.21, bf16[3,16,128,320]{2,3,1,0:T(8,128)(2,1)} %param.17, bf16[320,320]{1,0:T(8,128)(2,1)S(1)} %all_gather.12), kind=kOutput, calls=%fused_computation.27 | convolution fusion | flops 1275985920 | bytes 15933440 | tf_op jit(solution)/shard_map/bhwd,cd->bhwc/dot_general | solution.py:100
  178.1 5.7 %fusion.101 = f32[320,9,320]{0,2,1:T(8,128)S(1)} fusion(bf16[3,16,128,320]{2,3,1,0:T(8,128)(2,1)S(1)} %multiply_convert_fusion, bf16[3,18,130,320]{2,3,1,0:T(8,128)(2,1)} %get-tuple-element.13), kind=kOutput, calls=%fused_computation.110 | convolution fusion | flops 1258291200 | bytes 8355840 | tf_op jit(solution)/shard_map/bhwc,bhwd->cd/dot_general | solution.py:119
  183.8 1.3 collective-permute-start.2
  185.2 1.9 collective-permute-start.3
  187.1 5.5 %fusion.107 = f32[320,9,320]{0,2,1:T(8,128)S(1)} fusion(f32[320,9,320]{0,2,1:T(8,128)S(1)} %fusion.101, bf16[3,16,128,320]{2,3,1,0:T(8,128)(2,1)S(1)} %multiply_convert_fusion, bf16[3,18,130,320]{2,3,1,0:T(8,128)(2,1)} %get-tuple-element.13), kind=kOutput, calls=%fused_computation.112 | convolution fusion | flops 1258291200 | bytes 8355840 | tf_op jit(solution)/shard_map/bhwc,bhwd->cd/dot_general | solution.py:119
  192.6 2.3 fusion.113
  194.9 2.2 fusion.119
  197.1 2.3 fusion.125
  199.4 2.3 fusion.131
  201.7 2.2 fusion.137
  203.9 2.5 fusion.143
  206.4 2.3 fusion.149
  208.7 2.2 copy-done.10
  210.9 5.6 %copy.38 = f32[320,2880]{1,0:T(8,128)} copy(f32[320,2880]{0,1:T(8,128)} %bitcast.304) | data formatting | bytes 7372800 | tf_op jit(solution)/shard_map/reshape | solution.py:126
  216.5 7.6 %fusion.156 = f32[3,16,128,320]{2,3,1,0:T(8,128)} fusion(bf16[3,16,128,320]{2,3,1,0:T(8,128)(2,1)} %get-tuple-element.20, bf16[320,320]{1,0:T(8,128)(2,1)S(1)} %all_gather.12), kind=kOutput, calls=%fused_computation.151 | convolution fusion | flops 1258291200 | bytes 12001280 | tf_op jit(solution)/shard_map/bhwc,cd->bhwd/dot_general | solution.py:98
  224.1 2.2 convolution_bitcast_fusion
  226.3 2.3 pad_maximum_fusion
  228.8 9.0 %fusion.42 = f32[3,16,128,320]{2,3,1,0:T(8,128)} fusion(bf16[3,18,130,320]{2,3,1,0:T(8,128)(2,1)} %get-tuple-element.12, bf16[320,3,3,320]{3,0,2,1:T(8,128)(2,1)} %all-gather.3.cloned.1.call-done), kind=kOutput, calls=%fused_computation.57 | convolution fusion | flops 1258291200 | bytes 12042240 | tf_op jit(solution)/shard_map/bhwc,cd->bhwd/dot_general | solution.py:39
  237.7 7.5 %fusion.44 = f32[3,16,128,320]{2,3,1,0:T(8,128)} fusion(bf16[3,18,130,320]{2,3,1,0:T(8,128)(2,1)} %get-tuple-element.12, bf16[320,3,3,320]{3,0,2,1:T(8,128)(2,1)S(1)} %copy-done.11), kind=kOutput, calls=%fused_computation.59 | convolution fusion | flops 1258291200 | bytes 12042240 | tf_op jit(solution)/shard_map/bhwc,cd->bhwd/dot_general | solution.py:39
  245.3 5.5 %fusion.46 = f32[3,16,128,320]{2,3,1,0:T(8,128)} fusion(bf16[3,18,130,320]{2,3,1,0:T(8,128)(2,1)S(1)} %bitcast.299, bf16[320,3,3,320]{3,0,2,1:T(8,128)(2,1)S(1)} %copy-done.11), kind=kOutput, calls=%fused_computation.61 | convolution fusion | flops 1258291200 | bytes 12042240 | tf_op jit(solution)/shard_map/bhwc,cd->bhwd/dot_general | solution.py:39
  250.8 5.6 %fusion.48 = f32[3,16,128,320]{2,3,1,0:T(8,128)} fusion(bf16[3,18,130,320]{2,3,1,0:T(8,128)(2,1)S(1)} %bitcast.299, bf16[320,3,3,320]{3,0,2,1:T(8,128)(2,1)S(1)} %copy-done.11), kind=kOutput, calls=%fused_computation.63 | convolution fusion | flops 1258291200 | bytes 12042240 | tf_op jit(solution)/shard_map/bhwc,cd->bhwd/dot_general | solution.py:39
  256.4 5.3 %fusion.50 = f32[3,16,128,320]{2,3,1,0:T(8,128)} fusion(bf16[3,18,130,320]{2,3,1,0:T(8,128)(2,1)S(1)} %bitcast.299, bf16[320,3,3,320]{3,0,2,1:T(8,128)(2,1)S(1)} %copy-done.11), kind=kOutput, calls=%fused_computation.65 | convolution fusion | flops 1258291200 | bytes 12042240 | tf_op jit(solution)/shard_map/bhwc,cd->bhwd/dot_general | solution.py:39
  261.7 6.0 %fusion.52 = f32[3,16,128,320]{2,3,1,0:T(8,128)} fusion(bf16[3,18,130,320]{2,3,1,0:T(8,128)(2,1)S(1)} %bitcast.299, bf16[320,3,3,320]{3,0,2,1:T(8,128)(2,1)S(1)} %copy-done.11), kind=kOutput, calls=%fused_computation.67 | convolution fusion | flops 1258291200 | bytes 12042240 | tf_op jit(solution)/shard_map/bhwc,cd->bhwd/dot_general | solution.py:39
  267.7 5.5 %fusion.54 = f32[3,16,128,320]{2,3,1,0:T(8,128)} fusion(bf16[3,18,130,320]{2,3,1,0:T(8,128)(2,1)S(1)} %bitcast.299, bf16[320,3,3,320]{3,0,2,1:T(8,128)(2,1)S(1)} %copy-done.11), kind=kOutput, calls=%fused_computation.69 | convolution fusion | flops 1258291200 | bytes 12042240 | tf_op jit(solution)/shard_map/bhwc,cd->bhwd/dot_general | solution.py:39
  273.3 5.3 %fusion.56 = f32[3,16,128,320]{2,3,1,0:T(8,128)} fusion(bf16[3,18,130,320]{2,3,1,0:T(8,128)(2,1)S(1)} %bitcast.299, bf16[320,3,3,320]{3,0,2,1:T(8,128)(2,1)S(1)} %copy-done.11), kind=kOutput, calls=%fused_computation.71 | convolution fusion | flops 1258291200 | bytes 12042240 | tf_op jit(solution)/shard_map/bhwc,cd->bhwd/dot_general | solution.py:39
  278.6 28.7 %add_convert_fusion = bf16[3,16,128,320]{2,3,1,0:T(8,128)(2,1)} fusion(f32[3,16,128,320]{2,3,1,0:T(8,128)} %fusion.156, f32[3,16,128,320]{2,3,1,0:T(8,128)} %fusion.42, f32[3,16,128,320]{2,3,1,0:T(8,128)} %fusion.44, f32[3,16,128,320]{2,3,1,0:T(8,128)} %fusion.46, f32[3,16,128,320]{2,3,1,0:T(8,128)} %fusion.48, f32[3,16,128,320]{2,3,1,0:T(8,128)} %fusion.50, ...), kind=kOutput, calls=%fused_computation.28 | convolution fusion | flops 1287782400 | bytes 78892800 | tf_op jit(solution)/shard_map/bhwc,cd->bhwd/dot_general | solution.py:39
  307.3 7.6 %fusion.158 = f32[3,16,128,320]{2,3,1,0:T(8,128)} fusion(bf16[3,16,128,320]{2,3,1,0:T(8,128)(2,1)} %copy-done.3, bf16[320,3,3,320]{3,0,2,1:T(8,128)(2,1)S(1)} %copy-done.9), kind=kOutput, calls=%fused_computation.153 | convolution fusion | flops 1258291200 | bytes 12042240 | tf_op jit(solution)/shard_map/bhwd,cd->bhwc/dot_general | solution.py:54
  314.9 5.3 %fusion.19 = f32[3,16,128,320]{2,3,1,0:T(8,128)} fusion(bf16[3,1,128,320]{2,3,1,0:T(8,128)(2,1)S(1)} %collective-permute-done.3, bf16[3,16,128,320]{2,3,1,0:T(8,128)(2,1)S(1)} %copy-done.4, bf16[320,3,3,320]{3,0,2,1:T(8,128)(2,1)S(1)} %copy-done.9), kind=kOutput, calls=%fused_computation.33 | convolution fusion | flops 1266647040 | bytes 12288000 | tf_op jit(solution)/shard_map/bhwd,cd->bhwc/dot_general | solution.py:54
  320.2 5.3 %fusion.23 = f32[3,16,128,320]{2,3,1,0:T(8,128)} fusion(bf16[3,16,128,320]{2,3,1,0:T(8,128)(2,1)S(1)} %copy-done.4, bf16[3,1,128,320]{2,3,1,0:T(8,128)(2,1)S(1)} %collective-permute-done.2, bf16[320,3,3,320]{3,0,2,1:T(8,128)(2,1)S(1)} %copy-done.9), kind=kOutput, calls=%fused_computation.37 | convolution fusion | flops 1266647040 | bytes 12288000 | tf_op jit(solution)/shard_map/bhwd,cd->bhwc/dot_general | solution.py:54
  325.5 6.3 %fusion.9 = bf16[3,18,130,320]{2,3,1,0:T(8,128)(2,1)S(1)} fusion(bf16[3,1,128,320]{2,3,1,0:T(8,128)(2,1)S(1)} %collective-permute-done.3, bf16[3,16,128,320]{2,3,1,0:T(8,128)(2,1)S(1)} %copy-done.4, bf16[3,1,128,320]{2,3,1,0:T(8,128)(2,1)S(1)} %collective-permute-done.2), kind=kLoop, calls=%fused_computation.15 | loop fusion | flops 26956800 | bytes 8916480 | tf_op jit(solution)/shard_map/concatenate | solution.py:14
  331.9 5.5 %fusion.30 = f32[3,16,128,320]{2,3,1,0:T(8,128)} fusion(bf16[3,18,130,320]{2,3,1,0:T(8,128)(2,1)S(1)} %fusion.9, bf16[320,3,3,320]{3,0,2,1:T(8,128)(2,1)S(1)} %copy-done.9), kind=kOutput, calls=%fused_computation.45 | convolution fusion | flops 1258291200 | bytes 12042240 | tf_op jit(solution)/shard_map/bhwd,cd->bhwc/dot_general | solution.py:54
  337.4 5.3 %fusion.32 = f32[3,16,128,320]{2,3,1,0:T(8,128)} fusion(bf16[3,18,130,320]{2,3,1,0:T(8,128)(2,1)S(1)} %fusion.9, bf16[320,3,3,320]{3,0,2,1:T(8,128)(2,1)S(1)} %copy-done.9), kind=kOutput, calls=%fused_computation.47 | convolution fusion | flops 1258291200 | bytes 12042240 | tf_op jit(solution)/shard_map/bhwd,cd->bhwc/dot_general | solution.py:54
  342.8 5.5 %fusion.34 = f32[3,16,128,320]{2,3,1,0:T(8,128)} fusion(bf16[3,18,130,320]{2,3,1,0:T(8,128)(2,1)S(1)} %fusion.9, bf16[320,3,3,320]{3,0,2,1:T(8,128)(2,1)S(1)} %copy-done.9), kind=kOutput, calls=%fused_computation.49 | convolution fusion | flops 1258291200 | bytes 12042240 | tf_op jit(solution)/shard_map/bhwd,cd->bhwc/dot_general | solution.py:54
  348.3 5.4 %fusion.36 = f32[3,16,128,320]{2,3,1,0:T(8,128)} fusion(bf16[3,18,130,320]{2,3,1,0:T(8,128)(2,1)S(1)} %fusion.9, bf16[320,3,3,320]{3,0,2,1:T(8,128)(2,1)S(1)} %copy-done.9), kind=kOutput, calls=%fused_computation.51 | convolution fusion | flops 1258291200 | bytes 12042240 | tf_op jit(solution)/shard_map/bhwd,cd->bhwc/dot_general | solution.py:54
  353.7 5.4 %fusion.38 = f32[3,16,128,320]{2,3,1,0:T(8,128)} fusion(bf16[3,18,130,320]{2,3,1,0:T(8,128)(2,1)S(1)} %fusion.9, bf16[320,3,3,320]{3,0,2,1:T(8,128)(2,1)S(1)} %copy-done.9), kind=kOutput, calls=%fused_computation.53 | convolution fusion | flops 1258291200 | bytes 12042240 | tf_op jit(solution)/shard_map/bhwd,cd->bhwc/dot_general | solution.py:54
  359.1 5.3 %fusion.28 = f32[3,16,128,320]{2,3,1,0:T(8,128)} fusion(bf16[3,18,130,320]{2,3,1,0:T(8,128)(2,1)S(1)} %fusion.9, bf16[320,3,3,320]{3,0,2,1:T(8,128)(2,1)S(1)} %copy-done.9), kind=kOutput, calls=%fused_computation.43 | convolution fusion | flops 1258291200 | bytes 12042240 | tf_op jit(solution)/shard_map/bhwd,cd->bhwc/dot_general | solution.py:54
  364.5 24.3 %fusion.152 = f32[16,320]{1,0:T(8,128)S(1)} fusion(f32[3,16,128,320]{2,3,1,0:T(8,128)} %fusion.28, f32[3,16,128,320]{2,3,1,0:T(8,128)} %fusion.23, f32[3,16,128,320]{2,3,1,0:T(8,128)} %fusion.30, f32[3,16,128,320]{2,3,1,0:T(8,128)} %fusion.32, f32[3,16,128,320]{2,3,1,0:T(8,128)} %fusion.158, f32[3,16,128,320]{2,3,1,0:T(8,128)} %fusion.34, ...), kind=kOutput, calls=%fused_computation.128 | convolution fusion | flops 393314304 | bytes 70823936 | tf_op jit(solution)/shard_map/bhwr,bhwc->rc/dot_general | solution.py:109
  388.8 3.4 psum.22
  392.2 37.4 %psum.23 = f32[16,320]{1,0:T(8,128)} all-reduce(f32[16,320]{1,0:T(8,128)S(1)} %psum.22), channel_id=1, replica_groups=mesh['groups'=2,'mp'=8,'dp'=2] {'mp'}, use_global_device_ids=true, to_apply=%region_3.4 | all-reduce | flops 5120 | bytes 40960 | tf_op jit(solution)/shard_map/psum | solution.py:114
  429.6 1.1 slice.270
  430.6 0.4 reshape.23
  431.1 0.8 copy.48
  431.9 1.5 slice.271
  (61 shorter events, 0.4 us)
Async XLA Ops:
  7.2 62.4 %copy-start = (bf16[1280,320]{0,1:T(8,128)(2,1)S(1)}, bf16[1280,320]{0,1:T(8,128)(2,1)}, u32[]{:S(2)}) copy-start(bf16[1280,320]{0,1:T(8,128)(2,1)} %param.13) | copy-start | bytes 2457604
  7.2 87.6 %all-gather.5.cloned.1.call-start = ((), (), s32[]{:S(2)}) async-start(), calls=%async_computation.2 | async-start | bytes 2488320 | tf_op jit(solution)/shard_map/all_gather | solution.py:93
  7.9 11.8 %copy-start.13 = (bf16[40,320]{1,0:T(8,128)(2,1)S(1)}, bf16[40,320]{1,0:T(8,128)(2,1)}, u32[]{:S(2)}) copy-start(bf16[40,320]{1,0:T(8,128)(2,1)} %param.16) | copy-start | bytes 76804
  7.9 61.5 %copy-start.15 = (s32[3]{0:T(128)S(1)}, s32[3]{0:T(128)}, u32[]{:S(2)}) copy-start(s32[3]{0:T(128)} %param.11) | copy-start | bytes 40
  7.9 220.8 %all-gather.3.cloned.1.call-start = ((), (), s32[]{:S(2)}) async-start(), calls=%async_computation.1 | async-start | bytes 2488320 | tf_op jit(solution)/shard_map/all_gather | solution.py:90
  8.0 3.6 copy-start.5
  11.5 1.9 copy-start.6
  13.5 56.4 %collective-permute-start = (bf16[2,3,1,128,320]{3,4,2,1,0:T(8,128)(2,1)S(1)}, bf16[2,3,1,128,320]{3,4,2,1,0:T(8,128)(2,1)S(1)}, u32[]{:S(2)}, u32[]{:S(2)}) collective-permute-start(bf16[2,3,1,128,320]{3,4,2,1,0:T(8,128)(2,1)S(1)} %get-tuple-element.14), channel_id=1, source_target_pairs={{0,2},{2,4},{4,6},{6,8},{8,10},{10,12},{12,14},{1,3},{3,5},{5,7},{... | collective-permute-start | bytes 1474568 | tf_op jit(solution)/shard_map/ppermute | solution.py:16
  18.3 51.5 %collective-permute-start.1 = (bf16[2,3,1,128,320]{3,4,2,1,0:T(8,128)(2,1)S(1)}, bf16[2,3,1,128,320]{3,4,2,1,0:T(8,128)(2,1)S(1)}, u32[]{:S(2)}, u32[]{:S(2)}) collective-permute-start(bf16[2,3,1,128,320]{3,4,2,1,0:T(8,128)(2,1)S(1)} %get-tuple-element.15), channel_id=1, source_target_pairs={{2,0},{4,2},{6,4},{8,6},{10,8},{12,10},{14,12},{3,1},{5,3},{7,5},{... | collective-permute-start | bytes 1474568 | tf_op jit(solution)/shard_map/ppermute | solution.py:18
  19.7 344.8 %reduce-scatter.4.cloned.1.call-start = ((), (), s32[]{:S(2)}) async-start(), calls=%async_computation.4 | async-start | bytes 4608000
  94.8 9.1 %copy-start.2 = (bf16[3,18,130,320]{2,3,1,0:T(8,128)(2,1)S(1)}, bf16[3,18,130,320]{2,3,1,0:T(8,128)(2,1)}, u32[]{:S(2)}) copy-start(bf16[3,18,130,320]{2,3,1,0:T(8,128)(2,1)} %get-tuple-element.13) | copy-start | bytes 13478404
  94.8 9.1 %copy-start.9 = (bf16[320,3,3,320]{3,0,2,1:T(8,128)(2,1)S(1)}, bf16[320,3,3,320]{3,0,2,1:T(8,128)(2,1)}, u32[]{:S(2)}) copy-start(bf16[320,3,3,320]{3,0,2,1:T(8,128)(2,1)} %all-gather.5.cloned.1.call-done) | copy-start | bytes 5529604
  178.0 28.4 %copy-start.3 = (bf16[3,16,128,320]{2,3,1,0:T(8,128)(2,1)}, bf16[3,16,128,320]{2,3,1,0:T(8,128)(2,1)S(1)}, u32[]{:S(2)}) copy-start(bf16[3,16,128,320]{2,3,1,0:T(8,128)(2,1)S(1)} %multiply_convert_fusion) | copy-start | bytes 11796484
  178.1 14.5 %slice-start.3 = ((s8[8847360]{0:T(1024)(128)(4,1)}), s8[4194304]{0:T(1024)(128)(4,1)S(1)}, s32[]{:S(2)}) async-start(s8[8847360]{0:T(1024)(128)(4,1)} %bitcast.300), calls=%async_computation.8 | async-start | bytes 8388608
  178.1 14.5 %slice-start.4 = ((s8[8847360]{0:T(1024)(128)(4,1)}), s8[4194304]{0:T(1024)(128)(4,1)S(1)}, s32[]{:S(2)}) async-start(s8[8847360]{0:T(1024)(128)(4,1)} %bitcast.300), calls=%async_computation.9 | async-start | bytes 8388608
  183.8 136.4 %collective-permute-start.2 = (bf16[3,1,128,320]{2,3,1,0:T(8,128)(2,1)S(1)}, bf16[3,1,128,320]{2,3,1,0:T(8,128)(2,1)S(1)}, u32[]{:S(2)}, u32[]{:S(2)}) collective-permute-start(bf16[3,1,128,320]{2,3,1,0:T(8,128)(2,1)S(1)} %get-tuple-element.16), channel_id=1, source_target_pairs={{0,2},{2,4},{4,6},{6,8},{8,10},{10,12},{12,14},{1,3},{3,5},{5,7},{... | collective-permute-start | bytes 737288 | tf_op jit(solution)/shard_map/ppermute | solution.py:16
  185.2 7.5 %slice-start.5 = ((s8[8847360]{0:T(1024)(128)(4,1)}), s8[458752]{0:T(1024)(128)(4,1)S(1)}, s32[]{:S(2)}) async-start(s8[8847360]{0:T(1024)(128)(4,1)} %bitcast.300), calls=%async_computation.10 | async-start | bytes 917504
  185.2 129.7 %collective-permute-start.3 = (bf16[3,1,128,320]{2,3,1,0:T(8,128)(2,1)S(1)}, bf16[3,1,128,320]{2,3,1,0:T(8,128)(2,1)S(1)}, u32[]{:S(2)}, u32[]{:S(2)}) collective-permute-start(bf16[3,1,128,320]{2,3,1,0:T(8,128)(2,1)S(1)} %get-tuple-element.17), channel_id=1, source_target_pairs={{2,0},{4,2},{6,4},{8,6},{10,8},{12,10},{14,12},{3,1},{5,3},{7,5},{... | collective-permute-start | bytes 737288 | tf_op jit(solution)/shard_map/ppermute | solution.py:18
  208.7 2.2 copy-start.10
  216.5 7.6 %copy-start.7 = (bf16[3,16,128,320]{2,3,1,0:T(8,128)(2,1)S(1)}, bf16[3,16,128,320]{2,3,1,0:T(8,128)(2,1)}, u32[]{:S(2)}) copy-start(bf16[3,16,128,320]{2,3,1,0:T(8,128)(2,1)} %get-tuple-element.20) | copy-start | bytes 11796484
  216.5 7.6 %copy-start.14 = (bf16[3,16,128,320]{2,3,1,0:T(8,128)(2,1)S(1)}, bf16[3,16,128,320]{2,3,1,0:T(8,128)(2,1)}, u32[]{:S(2)}) copy-start(bf16[3,16,128,320]{2,3,1,0:T(8,128)(2,1)} %param.17) | copy-start | bytes 11796484
  224.1 2.2 copy-start.8
  228.7 200.9 %all-reduce.5.cloned.1.call-start = ((), (), s32[]{:S(2)}) async-start(), calls=%async_computation.3 | async-start | bytes 1024000 | tf_op jit(solution)/shard_map/psum | solution.py:130
  228.7 9.0 %copy-start.11 = (bf16[320,3,3,320]{3,0,2,1:T(8,128)(2,1)S(1)}, bf16[320,3,3,320]{3,0,2,1:T(8,128)(2,1)}, u32[]{:S(2)}) copy-start(bf16[320,3,3,320]{3,0,2,1:T(8,128)(2,1)} %all-gather.3.cloned.1.call-done) | copy-start | bytes 5529604
  228.7 16.5 %slice-start = ((s8[8847360]{0:T(1024)(128)(4,1)}), s8[4194304]{0:T(1024)(128)(4,1)S(1)}, s32[]{:S(2)}) async-start(s8[8847360]{0:T(1024)(128)(4,1)} %bitcast.298), calls=%async_computation.5 | async-start | bytes 8388608
  228.8 16.5 %slice-start.1 = ((s8[8847360]{0:T(1024)(128)(4,1)}), s8[4194304]{0:T(1024)(128)(4,1)S(1)}, s32[]{:S(2)}) async-start(s8[8847360]{0:T(1024)(128)(4,1)} %bitcast.298), calls=%async_computation.6 | async-start | bytes 8388608
  237.7 7.5 %slice-start.2 = ((s8[8847360]{0:T(1024)(128)(4,1)}), s8[458752]{0:T(1024)(128)(4,1)S(1)}, s32[]{:S(2)}) async-start(s8[8847360]{0:T(1024)(128)(4,1)} %bitcast.298), calls=%async_computation.7 | async-start | bytes 917504
  307.3 7.6 %copy-start.4 = (bf16[3,16,128,320]{2,3,1,0:T(8,128)(2,1)S(1)}, bf16[3,16,128,320]{2,3,1,0:T(8,128)(2,1)}, u32[]{:S(2)}) copy-start(bf16[3,16,128,320]{2,3,1,0:T(8,128)(2,1)} %copy-done.3) | copy-start | bytes 11796484
  359.1 5.4 %copy-start.12 = (s32[3,16,128]{2,1,0:T(8,128)S(1)}, s32[3,16,128]{2,1,0:T(8,128)}, u32[]{:S(2)}) copy-start(s32[3,16,128]{2,1,0:T(8,128)} %param.10) | copy-start | bytes 73732
  364.5 69.0 %copy-start.1 = (bf16[1280,320]{0,1:T(8,128)(2,1)S(1)}, bf16[1280,320]{0,1:T(8,128)(2,1)}, u32[]{:S(2)}) copy-start(bf16[1280,320]{0,1:T(8,128)(2,1)} %param.13) | copy-start | bytes 2457604
Sparse Core Ops, SparseCore 0:
  10.2 66.9 all-gather.4
  79.4 49.2 all-gather.2
  228.8 86.5 reduce-scatter.3
  364.6 19.8 all-reduce.4
